TPU v7x, 32 devices: a whole 2x2x4 slice. The times are simulated.
32 devices in a mesh: dp: 8 (over y, x, core), head: 4 (over z).
Axes of the slice: x: 2, y: 2, z: 4, core: 2. Of those that a mesh axis runs over, the one named last changes fastest.
Arguments:
- tokens: bfloat16 [8192, 8192], P('dp'), may hold values from -64 to 64
- w_query: bfloat16 [8192, 8192], P('dp', 'head'), may hold values from -0.0625 to 0.0625
- key_weight: bfloat16 [8192, 1024], P('dp', 'head'), may hold values from -0.0625 to 0.0625
- value_weight: bfloat16 [8192, 1024], P('dp', 'head'), may hold values from -0.0625 to 0.0625
- segment_ids: int32 [8192], P('dp'), may hold values from 0 to 27, as said below
Outputs:
- attended: bfloat16 [8192, 8192], P('dp', 'head')
Inputs may be any that keep to these rules, and one draw needn't show every extreme that they name: `segment_ids`: within each sequence of 1024 tokens the numbers start at 0 and never fall.
All inputs are finite; a program needn't handle non-finite values.
Results may differ from a plain program's by a relative error of at most 0.01.
The roundings to bfloat16 on the way count: a program that leaves them out, or rounds other values in their place, can miss the bound.
Values may be sent and summed in bfloat16 or wider, within the bound.
No kernel may reach another device: no remote copies, remote signals or barrier semaphores. Data moves between devices by JAX's collectives and lax.ppermute only.
A program may use at most 128 MiB of HBM per device.

v0:
```python
import jax
import jax.numpy as jnp
from jax import lax
from jax.sharding import PartitionSpec as P

QUERY_HEADS = 64
KEY_VALUE_HEADS = 8
HEAD_SIZE = 128
NBLK = 4


NEGATIVE = -1e30


def block_attend(queries, keys, values, segments, block):
    block_rows = queries.shape[0]
    heads_kv = queries.shape[1]
    grouped_heads = queries.shape[2]
    head_width = queries.shape[3]
    row_start = block * block_rows
    query_segments = segments[row_start : row_start + block_rows]
    query_positions = row_start + jnp.arange(block_rows, dtype=jnp.int32)
    inverse_root = 1.0 / jnp.sqrt(jnp.float32(head_width))

    def tile_update(state, column):
        running_max, denominator, weighted = state
        col_start = column * block_rows
        keys_tile = keys[col_start : col_start + block_rows]
        values_tile = values[col_start : col_start + block_rows]
        key_segments = segments[col_start : col_start + block_rows]
        key_positions = col_start + jnp.arange(block_rows, dtype=jnp.int32)
        mask = (key_positions[None, :] <= query_positions[:, None]) & (
            key_segments[None, :] == query_segments[:, None]
        )
        scores = (
            jnp.einsum("qhgd,khd->hgqk", queries, keys_tile, preferred_element_type=jnp.float32)
            * inverse_root
        )
        scores = jnp.where(mask, scores, NEGATIVE)
        new_max = jnp.maximum(running_max, jnp.max(scores, axis=3))
        weights = jnp.where(mask, jnp.exp(scores - new_max[..., None]), 0.0)
        fading = jnp.exp(running_max - new_max)
        denominator = denominator * fading + jnp.sum(weights, axis=3)
        weighted = weighted * fading[..., None] + jnp.einsum(
            "hgqk,khd->hgqd",
            weights.astype(jnp.bfloat16),
            values_tile,
            preferred_element_type=jnp.float32,
        )
        return (new_max, denominator, weighted)

    state = (
        jnp.full((heads_kv, grouped_heads, block_rows), NEGATIVE, jnp.float32),
        jnp.zeros((heads_kv, grouped_heads, block_rows), jnp.float32),
        jnp.zeros((heads_kv, grouped_heads, block_rows, head_width), jnp.float32),
    )
    for column in range(block + 1):
        if column == block:
            state = tile_update(state, column)
        else:
            needed = segments[row_start] == segments[column * block_rows + block_rows - 1]
            state = lax.cond(
                needed,
                lambda carried, column=column: tile_update(carried, column),
                lambda carried: carried,
                state,
            )
    result = state[2] / state[1][..., None]
    return (
        jnp.transpose(result, (2, 0, 1, 3))
        .reshape(block_rows, heads_kv * grouped_heads * head_width)
        .astype(jnp.bfloat16)
    )


def body(tokens, w_query, key_weight, value_weight, segment_ids):
    seq_rows = tokens.shape[0]

    def add_rows(piece):
        return jnp.dot(tokens, piece, preferred_element_type=jnp.float32)

    query_sum = add_rows(lax.all_gather(w_query, "dp", axis=0, tiled=True))
    key_sum = add_rows(lax.all_gather(key_weight, "dp", axis=0, tiled=True))
    value_sum = add_rows(lax.all_gather(value_weight, "dp", axis=0, tiled=True))
    heads_kv = key_weight.shape[1] // HEAD_SIZE
    grouped_heads = QUERY_HEADS // KEY_VALUE_HEADS
    queries = query_sum.astype(jnp.bfloat16).reshape(seq_rows, heads_kv, grouped_heads, HEAD_SIZE)
    keys = key_sum.astype(jnp.bfloat16).reshape(seq_rows, heads_kv, HEAD_SIZE)
    values = value_sum.astype(jnp.bfloat16).reshape(seq_rows, heads_kv, HEAD_SIZE)
    block_rows = seq_rows // NBLK
    pieces_out = [
        block_attend(
            queries[block * block_rows : (block + 1) * block_rows], keys, values, segment_ids, block
        )
        for block in range(NBLK)
    ]
    return jnp.concatenate(pieces_out, axis=0)


def solution(mesh):
    in_specs = (P("dp", None), P("dp", "head"), P("dp", "head"), P("dp", "head"), P("dp"))
    out_specs = P("dp", "head")
    return jax.shard_map(body, mesh=mesh, in_specs=in_specs, out_specs=out_specs, check_vma=False)
```

profile of v0, /device:TPU:3, one launch (start us, length us, event | category | flops | bytes accessed | tf_op | source)
XLA Modules:
  0.0 426.0 jit_solution(11183019970822498453)
XLA Ops:
  18.2 29.4 %all-gather.8.cloned.1.call-done = bf16[8192,256]{1,0:T(8,128)(2,1)} async-done(((bf16[1024,256]{1,0:T(8,128)(2,1)}), bf16[8192,256]{1,0:T(8,128)(2,1)}) %all-gather.8.cloned.1.call-update) | async-done | bytes 4194320 | tf_op jit(solution)/shard_map/all_gather | solution.py:84
  47.7 9.4 %convolution_convert_fusion.1 = bf16[1024,256]{0,1:T(8,128)(2,1)S(1)} fusion(bf16[1024,8192]{1,0:T(8,128)(2,1)} %param.17, bf16[8192,256]{1,0:T(8,128)(2,1)} %all-gather.8.cloned.1.call-done), kind=kOutput, calls=%fused_computation.194 | convolution fusion | flops 4295229440 | bytes 21495808 | tf_op jit(solution)/shard_map/dot_general | solution.py:80
  57.9 28.4 %all-gather.4.cloned.1.call-done = bf16[8192,256]{1,0:T(8,128)(2,1)} async-done(((bf16[1024,256]{1,0:T(8,128)(2,1)}), bf16[8192,256]{1,0:T(8,128)(2,1)}) %all-gather.4.cloned.1.call-update) | async-done | bytes 4194320 | tf_op jit(solution)/shard_map/all_gather | solution.py:83
  86.3 9.4 %convolution_convert_fusion.2 = bf16[1024,256]{0,1:T(8,128)(2,1)S(1)} fusion(bf16[1024,8192]{1,0:T(8,128)(2,1)} %param.17, bf16[8192,256]{1,0:T(8,128)(2,1)} %all-gather.4.cloned.1.call-done), kind=kOutput, calls=%fused_computation.195 | convolution fusion | flops 4295229440 | bytes 21495808 | tf_op jit(solution)/shard_map/dot_general | solution.py:80
  96.4 152.6 %all-gather.6.cloned.1.call-done = bf16[8192,2048]{1,0:T(8,128)(2,1)} async-done(((bf16[1024,2048]{1,0:T(8,128)(2,1)}), bf16[8192,2048]{1,0:T(8,128)(2,1)}) %all-gather.6.cloned.1.call-update) | async-done | bytes 33554448 | tf_op jit(solution)/shard_map/all_gather | solution.py:82
  249.0 51.6 %convolution_convert_fusion = bf16[1024,2048]{1,0:T(8,128)(2,1)S(1)} fusion(bf16[1024,8192]{1,0:T(8,128)(2,1)} %param.17, bf16[8192,2048]{1,0:T(8,128)(2,1)} %all-gather.6.cloned.1.call-done), kind=kOutput, calls=%fused_computation.151 | convolution fusion | flops 34361835520 | bytes 54525952 | tf_op jit(solution)/shard_map/dot_general | solution.py:80
  301.9 1.3 copy.94
  304.2 1.0 fusion.115
  305.2 2.3 fusion.132
  307.5 2.3 copy.45
  309.8 4.3 %fusion.112 = (f32[2,8,256]{2,1,0:T(8,128)S(1)}, f32[2,256,256,8]{2,1,3,0:T(8,128)}) fusion(pred[256,256]{0,1:T(8,128)(4,1)S(1)} %get-tuple-element.316, bf16[256,2,128,1]{0,2,3,1:T(8,128)(2,1)} %bitcast.330, bf16[256,2,8,128]{3,2,1,0:T(8,128)(2,1)} %bitcast.321), kind=kOutput, calls=%fused_computation.153 | convolution fusion | flops 271577088 | bytes 5455872 | tf_op jit(solution)/shard_map/qhgd,khd->hgqk/dot_general | solution.py:36
  314.1 14.1 %conditional.6 = (f32[2,8,256]{2,1,0:T(8,128)}, f32[2,8,256]{2,1,0:T(8,128)S(1)}, f32[2,8,256,128]{2,3,1,0:T(8,128)}) conditional(s32[]{:T(128)} %bitcast.40, () %tuple.47, (s32[256]{0:T(256)S(1)}, s32[1024]{0:T(1024)S(1)}, s32[256]{0:T(256)S(1)}, bf16[1024,2,128]{0,2,1:T(8,128)(2,1)S(1)}, bf16[256,2,8,128]{3,2,1,0:T(8,128)(2,1)}, ...), branch_computations={%region_2.3_spmd, %region_3.6_spmd} | conditional | flops 551239936 | bytes 22731800 | solution.py:62
  316.3 2.2 fusion
  319.1 1.7 fusion.2
  320.8 3.8 fusion.10
  324.6 2.9 copy.88
  329.1 3.6 fusion.117
  333.5 3.9 divide_convert_fusion.2
  337.5 2.3 copy.46
  339.7 11.1 %conditional.7 = (f32[2,8,256]{2,1,0:T(8,128)}, f32[2,8,256]{2,1,0:T(8,128)S(1)}, f32[2,8,256,128]{3,2,1,0:T(8,128)}) conditional(s32[]{:T(128)} %bitcast.52, () %tuple.49, (s32[256]{0:T(256)S(1)}, s32[1024]{0:T(1024)S(1)}, s32[256]{0:T(256)S(1)}, bf16[1024,2,128]{0,2,1:T(8,128)(2,1)S(1)}, bf16[256,2,8,128]{3,2,1,0:T(8,128)(2,1)S(1)}, ...), branch_computations={%region_8.9_spmd, %region_9.12_spmd} | conditional | flops 551239680 | bytes 18535448 | solution.py:62
  341.9 1.8 fusion.20
  344.3 1.7 fusion.22
  346.0 3.7 fusion.30
  350.9 14.1 %conditional.8 = (f32[2,8,256]{2,1,0:T(8,128)}, f32[2,8,256]{2,1,0:T(8,128)S(1)}, f32[2,8,256,128]{2,3,1,0:T(8,128)}) conditional(s32[]{:T(128)} %bitcast.51, (f32[2,8,256]{2,1,0:T(8,128)}, f32[2,8,256]{2,1,0:T(8,128)S(1)}, f32[2,8,256,128]{3,2,1,0:T(8,128)}) %conditional.7, (s32[256]{0:T(256)S(1)}, s32[1024]{0:T(1024)S(1)}, s32[256]{0:T(256)S(1)}, ...), branch_computations={%region_12.13_spmd, %region_13.16_spmd} | conditional | flops 551756032 | bytes 24910872 | solution.py:62
  353.1 1.8 fusion.40
  355.6 1.0 fusion.42
  357.4 4.1 multiply_add_fusion
  362.1 2.9 copy.90
  365.0 2.1 fusion.113
  367.7 1.0 fusion.119
  369.5 2.4 divide_convert_fusion.1
  371.9 1.5 copy.47
  373.4 10.8 %conditional.9 = (f32[2,8,256]{2,1,0:T(8,128)}, f32[2,8,256]{2,1,0:T(8,128)S(1)}, f32[2,8,256,128]{3,2,1,0:T(8,128)}) conditional(s32[]{:T(128)} %bitcast.63, () %tuple.52, (s32[256]{0:T(256)S(1)}, s32[1024]{0:T(1024)S(1)}, s32[256]{0:T(256)S(1)}, bf16[1024,2,128]{0,2,1:T(8,128)(2,1)S(1)}, bf16[256,2,8,128]{3,2,1,0:T(8,128)(2,1)S(1)}, ...), branch_computations={%region_18.19_spmd, %region_19.22_spmd} | conditional | flops 551239680 | bytes 18535448 | solution.py:62
  375.5 1.8 fusion.57
  377.9 1.7 fusion.59
  379.7 3.7 fusion.67
  384.1 11.3 %conditional.10 = ((f32[2,8,256]{2,1,0:T(8,128)}, f32[2,8,256]{2,1,0:T(8,128)S(1)}, f32[2,8,256,128]{3,2,1,0:T(8,128)})) conditional(s32[]{:T(128)} %bitcast.62, (f32[2,8,256]{2,1,0:T(8,128)}, f32[2,8,256]{2,1,0:T(8,128)S(1)}, f32[2,8,256,128]{3,2,1,0:T(8,128)}) %conditional.9, (s32[256]{0:T(256)S(1)}, s32[1024]{0:T(1024)S(1)}, s32[256]{0:T(256)S(1)}, ...), branch_computations={%region_22.23_spmd, %region_23.26_spmd} | conditional | flops 551756032 | bytes 20716576 | solution.py:62
  386.5 1.8 fusion.77
  389.0 1.0 fusion.79
  390.8 4.0 multiply_add_fusion.2
  395.4 12.4 %conditional.11 = (f32[2,8,256]{2,1,0:T(8,128)}, f32[2,8,256]{2,1,0:T(8,128)S(1)}, f32[2,8,256,128]{2,3,1,0:T(8,128)}) conditional(s32[]{:T(128)} %bitcast.61, (f32[2,8,256]{2,1,0:T(8,128)}, f32[2,8,256]{2,1,0:T(8,128)S(1)}, f32[2,8,256,128]{3,2,1,0:T(8,128)}) %get-tuple-element.353, (s32[256]{0:T(256)S(1)}, s32[1024]{0:T(1024)S(1)}, ...), branch_computations={%region_26.27_spmd, %region_27.30_spmd} | conditional | flops 551756032 | bytes 24910872 | solution.py:62
  398.5 1.0 fusion.96
  400.2 4.1 multiply_add_fusion.4
  404.9 2.9 copy.92
  409.6 1.0 fusion.121
  411.4 2.4 divide_convert_fusion
  413.7 2.3 copy.48
  416.0 3.3 pad_maximum_fusion
  (98 shorter events, 36.5 us)
Async XLA Ops:
  6.5 2.2 copy-start.11
  6.5 41.1 %all-gather.8.cloned.1.call-start = ((), (), s32[]{:S(2)}) async-start(), calls=%async_computation.2 | async-start | bytes 4718592 | tf_op jit(solution)/shard_map/all_gather | solution.py:84
  7.3 79.0 %all-gather.4.cloned.1.call-start = ((), (), s32[]{:S(2)}) async-start(), calls=%async_computation | async-start | bytes 4718592 | tf_op jit(solution)/shard_map/all_gather | solution.py:83
  8.0 241.0 %all-gather.6.cloned.1.call-start = ((), (), s32[]{:S(2)}) async-start(), calls=%async_computation.1 | async-start | bytes 37748736 | tf_op jit(solution)/shard_map/all_gather | solution.py:82
  301.2 2.0 copy-start.6
  303.2 2.1 copy-start.10
  328.2 5.3 %copy-start = (f32[2,256,256,8]{2,1,3,0:T(8,128)S(1)}, f32[2,256,256,8]{2,1,3,0:T(8,128)}, u32[]{:S(2)}) copy-start(f32[2,256,256,8]{2,1,3,0:T(8,128)} %get-tuple-element.310) | copy-start | bytes 12582916
  328.3 5.2 %copy-start.9 = (bf16[256,256]{0,1:T(8,128)(2,1)S(1)}, bf16[256,256]{0,1:T(8,128)(2,1)}, u32[]{:S(2)}) copy-start(bf16[256,256]{0,1:T(8,128)(2,1)} %get-tuple-element.288) | copy-start | bytes 393220
  364.9 4.5 %copy-start.3 = (f32[2,8,256,128]{2,3,1,0:T(8,128)S(1)}, f32[2,8,256,128]{2,3,1,0:T(8,128)}, u32[]{:S(2)}) copy-start(f32[2,8,256,128]{2,3,1,0:T(8,128)} %get-tuple-element.246) | copy-start | bytes 6291460
  364.9 4.6 %copy-start.8 = (bf16[256,256]{0,1:T(8,128)(2,1)S(1)}, bf16[256,256]{0,1:T(8,128)(2,1)}, u32[]{:S(2)}) copy-start(bf16[256,256]{0,1:T(8,128)(2,1)} %get-tuple-element.287) | copy-start | bytes 393220
  395.4 12.4 %copy-start.5 = (pred[256,256]{0,1:T(8,128)(4,1)S(1)}, pred[256,256]{0,1:T(8,128)(4,1)}, u32[]{:S(2)}) copy-start(pred[256,256]{0,1:T(8,128)(4,1)} %get-tuple-element.314) | copy-start | bytes 196612
  407.8 3.5 copy-start.4
  407.8 3.5 copy-start.7
  411.3 4.7 %copy-start.1 = (bf16[256,2048]{1,0:T(8,128)(2,1)S(1)}, bf16[256,2048]{1,0:T(8,128)(2,1)}, u32[]{:S(2)}) copy-start(bf16[256,2048]{1,0:T(8,128)(2,1)} %copy.45) | copy-start | bytes 3145732
  411.3 4.7 %copy-start.2 = (bf16[256,2048]{1,0:T(8,128)(2,1)S(1)}, bf16[256,2048]{1,0:T(8,128)(2,1)}, u32[]{:S(2)}) copy-start(bf16[256,2048]{1,0:T(8,128)(2,1)} %copy.46) | copy-start | bytes 3145732
Sparse Core Ops, SparseCore 0:
  9.2 38.3 all-gather.7
  49.5 36.7 all-gather.3
  88.2 160.7 all-gather.5
where the time goes:
time: 432 us; the launch traced here: 426 us
  waiting for transfers between devices  213 us (49%)
  matrix products  123 us (28%)
  local copies, waits for them, and re-layouts  34.9 us (8%)
  other arithmetic  32.9 us (8%)
  between operations  21.3 us (5%)
    all_gather x1, waiting for transfers between devices, body(): query_sum = add_rows(lax.all_gather(w_query, 'dp', axis=0, tiled=True))  153 us
    dot_general x3, matrix products, add_rows(): return jnp.dot(tokens, piece, preferred_element_type=jnp.float32)  70.3 us
    dot_general x10, matrix products, tile_update(): jnp.einsum('hgqk,khd->hgqd', weights.astype(jnp.bfloat16), values_tile, p...  34.4 us
    all_gather x1, waiting for transfers between devices, body(): value_sum = add_rows(lax.all_gather(value_weight, 'dp', axis=0, tiled=True))  29.4 us
    all_gather x1, waiting for transfers between devices, body(): key_sum = add_rows(lax.all_gather(key_weight, 'dp', axis=0, tiled=True))  28.4 us
    dot_general x10, matrix products, tile_update(): jnp.einsum('qhgd,khd->hgqk', queries, keys_tile, preferred_element_type=j...  18.8 us
    reduce_sum x10, other arithmetic, tile_update(): denominator = denominator * fading + jnp.sum(weights, axis=3)  14.9 us
    another operation x12, local copies, waits for them, and re-layouts  11.3 us
  transfers between devices with their start and end apart: 3, of which 3 were waited for; matrix products, arithmetic and copies ran while one was open for 5% of the time, Pallas kernels for 0%

commit v1 on v0

v1 whole, which is shorter than its diff:
```python
import functools
import math

import jax
import jax.numpy as jnp
from jax import lax
from jax.experimental import pallas as pl
from jax.experimental.pallas import tpu as pltpu
from jax.sharding import PartitionSpec as P

QUERY_HEADS = 64
KEY_VALUE_HEADS = 8
HEAD_SIZE = 128
GROUP = QUERY_HEADS // KEY_VALUE_HEADS
CHUNK = 256
ROW_BLOCK = 256
NEGATIVE = -1e30
VMEM_BYTES = 56 * 1024 * 1024


def ring_of(n_dp):
    chips = n_dp // 2
    half = chips // 2
    return list(range(half)) + list(range(chips - 1, half - 1, -1))


def shift_pairs(n_dp, step):
    ring = ring_of(n_dp)
    size = len(ring)
    return [
        (ring[at] * 2 + core, ring[(at + step) % size] * 2 + core)
        for at in range(size)
        for core in range(2)
    ]


def attend_rows(query, keys, values, allowed):
    scale = math.log2(math.e) / math.sqrt(HEAD_SIZE)
    scores = lax.dot_general(query, keys, (((1,), (1,)), ((), ())), preferred_element_type=jnp.float32)
    scores = jnp.where(allowed, scores, NEGATIVE)
    top = jnp.max(scores, axis=1, keepdims=True)
    weights = jnp.exp2((scores - top) * scale)
    denominator = jnp.sum(weights, axis=1, keepdims=True)
    summed = jnp.dot(weights.astype(jnp.bfloat16), values, preferred_element_type=jnp.float32)
    return (summed / denominator).astype(jnp.bfloat16)


def attend_chunk(query, key_ref, value_ref, seg_row_ref, seg_col_ref, out_ref):
    rows = query.shape[0]
    heads = query.shape[1] // HEAD_SIZE
    for start in range(0, rows, ROW_BLOCK):
        stop = min(start + ROW_BLOCK, rows)
        seg_q = seg_col_ref[start:stop, :]
        seg_k = seg_row_ref[:, :stop]
        at_q = start + lax.broadcasted_iota(jnp.int32, (stop - start, stop), 0)
        at_k = lax.broadcasted_iota(jnp.int32, (stop - start, stop), 1)
        allowed = (seg_q == seg_k) & (at_k <= at_q)
        for head in range(heads):
            columns = slice(head * HEAD_SIZE, (head + 1) * HEAD_SIZE)
            out_ref[start:stop, columns] = attend_rows(
                query[start:stop, columns], key_ref[:stop, :], value_ref[:stop, :], allowed
            )


def project_kernel(n_pieces, has_start, mode, order_ref, tokens_ref, *refs):
    pieces = refs[:n_pieces]
    refs = refs[n_pieces:]
    start_ref = None
    if has_start:
        start_ref, refs = refs[0], refs[1:]
    if mode == "attend":
        key_ref, value_ref, seg_row_ref, seg_col_ref = refs[:4]
        out_ref, total = refs[-2:]
    elif mode == "partial":
        (out_ref,) = refs
        total = out_ref
    else:
        out_ref, total = refs
    step = pl.program_id(0)
    for at, piece in enumerate(pieces):

        @pl.when(step == at)
        def _(at=at, piece=piece):
            part = jnp.dot(tokens_ref[...], piece[...], preferred_element_type=jnp.float32)
            if at > 0:
                part = part + total[...]
            elif has_start:
                part = part + start_ref[...]
            if at < n_pieces - 1 or mode == "partial":
                total[...] = part
            elif mode == "round":
                out_ref[...] = part.astype(jnp.bfloat16)
            else:
                attend_chunk(
                    part.astype(jnp.bfloat16), key_ref, value_ref, seg_row_ref, seg_col_ref, out_ref
                )


def project(tokens, order, pieces, width, mode, start=None, attention=None, name=None):
    rows = tokens.shape[0]
    depth = pieces[0][0].shape[0]
    n_pieces = len(pieces)
    whole = lambda step, order: (0, 0)
    in_specs = [pl.BlockSpec((rows, depth), lambda step, order: (0, order[step]))]
    args = [tokens]
    for array, block in pieces:
        in_specs.append(pl.BlockSpec((depth, width), lambda step, order, block=block: (0, block)))
        args.append(array)
    if start is not None:
        in_specs.append(pl.BlockSpec((rows, width), whole))
        args.append(start)
    scratch = [pltpu.VMEM((rows, width), jnp.float32)]
    aliases = {}
    flops = 2 * rows * depth * n_pieces * width
    if mode == "attend":
        keys, values, kv_block, seg_row, seg_col, out, column, out_columns = attention
        kv_spec = pl.BlockSpec((rows, HEAD_SIZE), lambda step, order: (0, kv_block))
        in_specs += [kv_spec, kv_spec, pl.BlockSpec(seg_row.shape, whole), pl.BlockSpec(seg_col.shape, whole)]
        args += [keys, values, seg_row, seg_col]
        if out is not None:
            in_specs.append(pl.BlockSpec(memory_space=pl.ANY))
            args.append(out)
            aliases = {len(args): 0}
        out_shape = jax.ShapeDtypeStruct((rows, out_columns), jnp.bfloat16)
        out_spec = pl.BlockSpec((rows, width), lambda step, order: (0, column))
        flops += 4 * rows * rows * width
    elif mode == "partial":
        scratch = []
        out_shape = jax.ShapeDtypeStruct((rows, width), jnp.float32)
        out_spec = pl.BlockSpec((rows, width), whole)
    else:
        out_shape = jax.ShapeDtypeStruct((rows, width), jnp.bfloat16)
        out_spec = pl.BlockSpec((rows, width), whole)
    return pl.pallas_call(
        functools.partial(project_kernel, n_pieces, start is not None, mode),
        grid_spec=pltpu.PrefetchScalarGridSpec(
            num_scalar_prefetch=1,
            grid=(n_pieces,),
            in_specs=in_specs,
            out_specs=out_spec,
            scratch_shapes=scratch,
        ),
        out_shape=out_shape,
        input_output_aliases=aliases,
        compiler_params=pltpu.CompilerParams(
            dimension_semantics=("arbitrary",), vmem_limit_bytes=VMEM_BYTES
        ),
        cost_estimate=pl.CostEstimate(
            flops=flops, bytes_accessed=2 * rows * depth * n_pieces, transcendentals=0
        ),
        name=name,
    )(order, *args)


def body(tokens, w_query, key_weight, value_weight, segment_ids):
    n_dp = lax.axis_size("dp")
    ring = ring_of(n_dp)
    size = len(ring)
    hops = size // 2
    right = functools.partial(lax.ppermute, axis_name="dp", perm=shift_pairs(n_dp, 1))
    left = functools.partial(lax.ppermute, axis_name="dp", perm=shift_pairs(n_dp, -1))
    sibling = functools.partial(lax.ppermute, axis_name="dp", perm=[(at, at ^ 1) for at in range(n_dp)])

    tables = {"whole": [], "split": [], "early": [], "late": []}
    for device in range(n_dp):
        at, core = ring.index(device // 2), device % 2
        near = [at]
        for hop in range(1, hops):
            near += [(at - hop) % size, (at + hop) % size]
        far = (at + hops) % size
        early = [ring[chip] * 2 + (core ^ other) for chip in near for other in range(2)]
        late = [ring[far] * 2 + (core ^ other) for other in range(2)]
        tables["early"].append(early)
        tables["whole"].append(early + late)
        tables["late"].append([late[0] * 2, late[0] * 2 + 1, late[1] * 2, late[1] * 2 + 1])
    me = lax.axis_index("dp")
    order = {
        kind: jnp.asarray(tables[kind], jnp.int32)[me] for kind in ("early", "whole", "late")
    }

    def gather(piece, mode):
        near = []
        from_left = from_right = piece
        for _ in range(1, hops):
            from_left, from_right = right(from_left), left(from_right)
            near += [from_left, sibling(from_left), from_right, sibling(from_right)]
        if mode == "right":
            far = [right(from_left)]
        elif mode == "left":
            far = [left(from_right)]
        else:
            middle = piece.shape[0] // 2
            far = [right(from_left[:middle]), left(from_right[middle:])]
        return near, far + [sibling(part) for part in far]

    key_sibling, value_sibling = sibling(key_weight), sibling(value_weight)
    key_near, key_far = gather(key_weight, "right")
    value_near, value_far = gather(value_weight, "left")
    query_sibling = sibling(w_query)

    def paired(arrays, block=0):
        return [(array, block) for array in arrays]

    kv_width = key_weight.shape[1]
    keys = project(
        tokens, order["whole"], paired([key_weight, key_sibling] + key_near + key_far), kv_width, "round", name="project_keys"
    )
    values = project(
        tokens, order["whole"], paired([value_weight, value_sibling] + value_near + value_far), kv_width, "round", name="project_values"
    )
    seg_row = segment_ids.reshape(1, -1)
    seg_col = segment_ids.reshape(-1, 1)

    columns = w_query.shape[1]
    out = None
    n_chunks = columns // CHUNK
    for chunk in range(n_chunks):
        mode = "split" if chunk >= n_chunks - 2 else ("right", "left")[chunk % 2]
        piece = w_query[:, chunk * CHUNK : (chunk + 1) * CHUNK]
        near, far = gather(piece, mode)
        local = paired([w_query, query_sibling], chunk) + paired(near)
        kv_block = chunk * CHUNK // (GROUP * HEAD_SIZE)
        attention = (keys, values, kv_block, seg_row, seg_col, out, chunk, columns)
        if mode == "split":
            start = project(tokens, order["early"], local, CHUNK, "partial", name="project_near")
            out = project(tokens, order["late"], paired(far), CHUNK, "attend", start, attention, name="project_far_attend")
        else:
            out = project(tokens, order["whole"], local + paired(far), CHUNK, "attend", None, attention, name="project_attend")
    return out


def solution(mesh):
    in_specs = (P("dp", None), P("dp", "head"), P("dp", "head"), P("dp", "head"), P("dp"))
    out_specs = P("dp", "head")
    return jax.shard_map(body, mesh=mesh, in_specs=in_specs, out_specs=out_specs, check_vma=False)
```

time: 432 us -> 366 us (0.85)
  the two profiles are of different devices: /device:TPU:3 before, /device:TPU:0 now
where the time goes in v1:
time: 366 us; the launch traced here: 361 us
  Pallas kernels  174 us (48%)
  waiting for transfers between devices  118 us (32%)
  starting transfers between devices  52.3 us (14%)
  local copies, waits for them, and re-layouts  15 us (4%)
    pallas_call x12, Pallas kernels, project(): pl.pallas_call(functools.partial(project_kernel, n_pieces, start is not N...  174 us
    ppermute x20, waiting for transfers between devices, gather(): from_left, from_right = (right(from_left), left(from_right))  86.7 us
    ppermute x20, starting transfers between devices, gather(): from_left, from_right = (right(from_left), left(from_right))  24.8 us
    ppermute x4, waiting for transfers between devices, gather(): far = [right(from_left)]  11.1 us
    ppermute x4, waiting for transfers between devices, gather(): far = [left(from_right)]  10.9 us
    ppermute x4, waiting for transfers between devices, gather(): far = [right(from_left[:middle]), left(from_right[middle:])]  9.58 us
    ppermute x4, starting transfers between devices, gather(): far = [left(from_right)]  7.39 us
  transfers between devices with their start and end apart: 67, of which 19 were waited for; matrix products, arithmetic and copies ran while one was open for 2% of the time, Pallas kernels for 46%

profile of v1, /device:TPU:0, one launch (start us, length us, event | category | flops | bytes accessed | tf_op | source)
XLA Modules:
  0.0 360.5 jit_solution(3041901001989327390)
XLA Ops:
  0.0 2.9 collective-permute-start.10
  3.0 2.0 collective-permute-start.19
  5.1 2.5 fusion.3
  7.5 8.4 %collective-permute-done.10.refs_2_ = bf16[1024,256]{1,0:T(8,128)(2,1)S(1)} collective-permute-done((bf16[1024,256]{1,0:T(8,128)(2,1)}, bf16[1024,256]{1,0:T(8,128)(2,1)S(1)}, u32[]{:S(2)}, u32[]{:S(2)}) %collective-permute-start.10) | collective-permute-done | bytes 524320 | tf_op jit(solution)/shard_map/ppermute | solution.py:185
  15.9 2.1 collective-permute-done.12.refs_4_
  20.0 9.2 %collective-permute-done.19.refs_4_ = bf16[1024,256]{1,0:T(8,128)(2,1)S(1)} collective-permute-done((bf16[1024,256]{1,0:T(8,128)(2,1)}, bf16[1024,256]{1,0:T(8,128)(2,1)S(1)}, u32[]{:S(2)}, u32[]{:S(2)}) %collective-permute-start.19) | collective-permute-done | bytes 524320 | tf_op jit(solution)/shard_map/ppermute | solution.py:185
  29.3 2.0 collective-permute-start.55
  31.3 1.5 collective-permute-start.49
  32.8 5.6 %collective-permute-done.61.refs_2_ = bf16[1024,256]{1,0:T(8,128)(2,1)S(1)} collective-permute-done((bf16[1024,256]{1,0:T(8,128)(2,1)S(1)}, bf16[1024,256]{1,0:T(8,128)(2,1)S(1)}, u32[]{:S(2)}, u32[]{:S(2)}) %collective-permute-start.61) | collective-permute-done | bytes 524320 | tf_op jit(solution)/shard_map/ppermute | solution.py:185
  38.4 2.1 collective-permute-start.51
  42.0 9.7 %collective-permute-done.57.refs_4_ = bf16[1024,256]{1,0:T(8,128)(2,1)S(1)} collective-permute-done((bf16[1024,256]{1,0:T(8,128)(2,1)S(1)}, bf16[1024,256]{1,0:T(8,128)(2,1)S(1)}, u32[]{:S(2)}, u32[]{:S(2)}) %collective-permute-start.57) | collective-permute-done | bytes 524320 | tf_op jit(solution)/shard_map/ppermute | solution.py:185
  53.2 7.7 %collective-permute-done.49.refs_2_ = bf16[1024,256]{1,0:T(8,128)(2,1)} collective-permute-done((bf16[1024,256]{1,0:T(8,128)(2,1)S(1)}, bf16[1024,256]{1,0:T(8,128)(2,1)}, u32[]{:S(2)}, u32[]{:S(2)}) %collective-permute-start.49) | collective-permute-done | bytes 524320 | tf_op jit(solution)/shard_map/ppermute | solution.py:185
  61.0 2.0 collective-permute-start.37
  63.1 11.1 %collective-permute-done.45.refs_4_ = bf16[1024,256]{1,0:T(8,128)(2,1)S(1)} collective-permute-done((bf16[1024,256]{1,0:T(8,128)(2,1)S(1)}, bf16[1024,256]{1,0:T(8,128)(2,1)S(1)}, u32[]{:S(2)}, u32[]{:S(2)}) %collective-permute-start.45) | collective-permute-done | bytes 524320 | tf_op jit(solution)/shard_map/ppermute | solution.py:185
  74.2 2.0 collective-permute-start.23
  76.3 7.1 %collective-permute-done.37.refs_2_ = bf16[1024,256]{1,0:T(8,128)(2,1)S(1)} collective-permute-done((bf16[1024,256]{1,0:T(8,128)(2,1)S(1)}, bf16[1024,256]{1,0:T(8,128)(2,1)S(1)}, u32[]{:S(2)}, u32[]{:S(2)}) %collective-permute-start.37) | collective-permute-done | bytes 524320 | tf_op jit(solution)/shard_map/ppermute | solution.py:185
  83.3 2.0 collective-permute-start.31
  86.2 10.4 %collective-permute-done.33.refs_4_ = bf16[1024,256]{1,0:T(8,128)(2,1)S(1)} collective-permute-done((bf16[1024,256]{1,0:T(8,128)(2,1)S(1)}, bf16[1024,256]{1,0:T(8,128)(2,1)S(1)}, u32[]{:S(2)}, u32[]{:S(2)}) %collective-permute-start.33) | collective-permute-done | bytes 524320 | tf_op jit(solution)/shard_map/ppermute | solution.py:185
  98.8 7.0 %collective-permute-done.31.refs_2_ = bf16[1024,256]{1,0:T(8,128)(2,1)S(1)} collective-permute-done((bf16[1024,256]{1,0:T(8,128)(2,1)S(1)}, bf16[1024,256]{1,0:T(8,128)(2,1)S(1)}, u32[]{:S(2)}, u32[]{:S(2)}) %collective-permute-start.31) | collective-permute-done | bytes 524320 | tf_op jit(solution)/shard_map/ppermute | solution.py:185
  105.8 2.0 collective-permute-start.24
  109.4 7.6 %collective-permute-done.refs_2_ = bf16[1024,256]{1,0:T(8,128)(2,1)S(1)} collective-permute-done((bf16[1024,256]{1,0:T(8,128)(2,1)S(1)}, bf16[1024,256]{1,0:T(8,128)(2,1)S(1)}, u32[]{:S(2)}, u32[]{:S(2)}) %collective-permute-start) | collective-permute-done | bytes 524320 | tf_op jit(solution)/shard_map/ppermute | solution.py:185
  117.7 5.0 %collective-permute-done.24.refs_0_ = bf16[512,256]{1,0:T(8,128)(2,1)S(1)} collective-permute-done((bf16[512,256]{1,0:T(8,128)(2,1)S(1)}, bf16[512,256]{1,0:T(8,128)(2,1)S(1)}, u32[]{:S(2)}, u32[]{:S(2)}) %collective-permute-start.24) | collective-permute-done | bytes 262176 | tf_op jit(solution)/shard_map/ppermute | solution.py:193
  122.7 2.1 collective-permute-start.26
  124.7 4.6 %collective-permute-done.26.refs_1_ = bf16[512,256]{1,0:T(8,128)(2,1)S(1)} collective-permute-done((bf16[512,256]{1,0:T(8,128)(2,1)S(1)}, bf16[512,256]{1,0:T(8,128)(2,1)S(1)}, u32[]{:S(2)}, u32[]{:S(2)}) %collective-permute-start.26) | collective-permute-done | bytes 262176 | tf_op jit(solution)/shard_map/ppermute | solution.py:193
  129.3 2.0 collective-permute-start.21
  131.4 1.8 collective-permute-done.14.refs_6_
  133.7 1.7 collective-permute-start.65
  135.4 5.5 %collective-permute-done.21.refs_6_ = bf16[1024,256]{1,0:T(8,128)(2,1)} collective-permute-done((bf16[1024,256]{1,0:T(8,128)(2,1)S(1)}, bf16[1024,256]{1,0:T(8,128)(2,1)}, u32[]{:S(2)}, u32[]{:S(2)}) %collective-permute-start.21) | collective-permute-done | bytes 524320 | tf_op jit(solution)/shard_map/ppermute | solution.py:190
  141.4 1.5 collective-permute-start.59
  143.0 4.7 %collective-permute-done.65.refs_6_ = bf16[1024,256]{1,0:T(8,128)(2,1)} collective-permute-done((bf16[1024,256]{1,0:T(8,128)(2,1)S(1)}, bf16[1024,256]{1,0:T(8,128)(2,1)}, u32[]{:S(2)}, u32[]{:S(2)}) %collective-permute-start.65) | collective-permute-done | bytes 524320 | tf_op jit(solution)/shard_map/ppermute | solution.py:188
  148.2 1.7 collective-permute-start.53
  149.9 5.4 %collective-permute-done.59.refs_6_ = bf16[1024,256]{1,0:T(8,128)(2,1)S(1)} collective-permute-done((bf16[1024,256]{1,0:T(8,128)(2,1)S(1)}, bf16[1024,256]{1,0:T(8,128)(2,1)S(1)}, u32[]{:S(2)}, u32[]{:S(2)}) %collective-permute-start.59) | collective-permute-done | bytes 524320 | tf_op jit(solution)/shard_map/ppermute | solution.py:190
  157.9 4.6 %collective-permute-done.53.refs_6_ = bf16[1024,256]{1,0:T(8,128)(2,1)} collective-permute-done((bf16[1024,256]{1,0:T(8,128)(2,1)}, bf16[1024,256]{1,0:T(8,128)(2,1)}, u32[]{:S(2)}, u32[]{:S(2)}) %collective-permute-start.53) | collective-permute-done | bytes 524320 | tf_op jit(solution)/shard_map/ppermute | solution.py:188
  162.5 1.9 collective-permute-start.47
  169.9 13.2 %project_keys.1.refs_8_.refs_5_ = bf16[1024,256]{1,0:T(8,128)(2,1)} custom-call(s32[8]{0:T(128)} %fusion.2.order_ref, bf16[1024,8192]{1,0:T(8,128)(2,1)} %tokens_ref.23, bf16[1024,256]{1,0:T(8,128)(2,1)} %refs_0_.11, bf16[1024,256]{1,0:T(8,128)(2,1)} %copy-done.40, bf16[1024,256]{1,0:T(8,128)(2,1)} %copy-done.37, bf16[1024,256]{1,0:T(8,128)(2,1)} %copy-done.41, ...), custom_call_target="tpu_custom_call" | custom-call | flops 4294967296 | bytes 16777216 | tf_op jit(solution)/shard_map/project_keys/pallas_call | solution.py:134
  183.9 13.3 %project_values.1.refs_9_.refs_6_ = bf16[1024,256]{1,0:T(8,128)(2,1)} custom-call(s32[8]{0:T(128)} %fusion.2.order_ref, bf16[1024,8192]{1,0:T(8,128)(2,1)} %tokens_ref.23, bf16[1024,256]{1,0:T(8,128)(2,1)} %refs_0_.12, bf16[1024,256]{1,0:T(8,128)(2,1)} %copy-done.38, bf16[1024,256]{1,0:T(8,128)(2,1)} %copy-done.36, ...), custom_call_target="tpu_custom_call" | custom-call | flops 4294967296 | bytes 16777216 | tf_op jit(solution)/shard_map/project_values/pallas_call | solution.py:134
  198.0 17.5 %project_attend.6.refs_12_ = bf16[1024,2048]{1,0:T(8,128)(2,1)} custom-call(s32[8]{0:T(128)} %fusion.2.order_ref, bf16[1024,8192]{1,0:T(8,128)(2,1)} %tokens_ref.23, bf16[1024,2048]{1,0:T(8,128)(2,1)} %refs_0_.19, bf16[1024,2048]{1,0:T(8,128)(2,1)} %collective-permute-done.6.refs_1_, bf16[1024,256]{1,0:T(8,128)(2,1)} %copy-done.16, ...), custom_call_target="tpu_custom_call" | custom-call | flops 5368709120 | bytes 16777216 | tf_op jit(solution)/shard_map/project_attend/pallas_call | solution.py:134
  215.9 1.9 collective-permute-start.35
  217.8 17.6 %project_attend.7.refs_12_ = bf16[1024,2048]{1,0:T(8,128)(2,1)} custom-call(s32[8]{0:T(128)} %fusion.2.order_ref, bf16[1024,8192]{1,0:T(8,128)(2,1)} %tokens_ref.23, bf16[1024,2048]{1,0:T(8,128)(2,1)} %refs_0_.19, bf16[1024,2048]{1,0:T(8,128)(2,1)} %collective-permute-done.6.refs_1_, ...), custom_call_target="tpu_custom_call", output_to_operand_aliasing={{}: (14, {})} | custom-call | flops 5368709120 | bytes 16777216 | tf_op jit(solution)/shard_map/project_attend/pallas_call | solution.py:134
  236.1 18.0 %project_attend.8.refs_12_ = bf16[1024,2048]{1,0:T(8,128)(2,1)} custom-call(s32[8]{0:T(128)} %fusion.2.order_ref, bf16[1024,8192]{1,0:T(8,128)(2,1)} %tokens_ref.23, bf16[1024,2048]{1,0:T(8,128)(2,1)} %refs_0_.19, bf16[1024,2048]{1,0:T(8,128)(2,1)} %collective-permute-done.6.refs_1_, ...), custom_call_target="tpu_custom_call", output_to_operand_aliasing={{}: (14, {})} | custom-call | flops 5368709120 | bytes 16777216 | tf_op jit(solution)/shard_map/project_attend/pallas_call | solution.py:134
  255.6 17.7 %project_attend.9.refs_12_ = bf16[1024,2048]{1,0:T(8,128)(2,1)} custom-call(s32[8]{0:T(128)} %fusion.2.order_ref, bf16[1024,8192]{1,0:T(8,128)(2,1)} %tokens_ref.23, bf16[1024,2048]{1,0:T(8,128)(2,1)} %refs_0_.19, bf16[1024,2048]{1,0:T(8,128)(2,1)} %collective-permute-done.6.refs_1_, bf16[1024,256]{1,0:T(8,128)(2,1)} %copy-done.10, ...), custom_call_target="tpu_custom_call", output_to_operand_aliasing={{}: (14, {})} | custom-call | flops 5368709120 | bytes 16777216 | tf_op jit(solution)/shard_map/project_attend/pallas_call | solution.py:134
  274.1 17.7 %project_attend.10.refs_12_ = bf16[1024,2048]{1,0:T(8,128)(2,1)} custom-call(s32[8]{0:T(128)} %fusion.2.order_ref, bf16[1024,8192]{1,0:T(8,128)(2,1)} %tokens_ref.23, bf16[1024,2048]{1,0:T(8,128)(2,1)} %refs_0_.19, bf16[1024,2048]{1,0:T(8,128)(2,1)} %collective-permute-done.6.refs_1_, bf16[1024,256]{1,0:T(8,128)(2,1)} %copy-done.6, ...), custom_call_target="tpu_custom_call", output_to_operand_aliasing={{}: (14, {})} | custom-call | flops 5368709120 | bytes 16777216 | tf_op jit(solution)/shard_map/project_attend/pallas_call | solution.py:134
  293.3 17.8 %project_attend.11.refs_9_ = bf16[1024,2048]{1,0:T(8,128)(2,1)} custom-call(s32[8]{0:T(128)} %fusion.2.order_ref, bf16[1024,8192]{1,0:T(8,128)(2,1)} %tokens_ref.23, bf16[1024,2048]{1,0:T(8,128)(2,1)} %refs_0_.19, bf16[1024,2048]{1,0:T(8,128)(2,1)} %collective-permute-done.6.refs_1_, bf16[1024,256]{1,0:T(8,128)(2,1)} %copy-done.8, ...), custom_call_target="tpu_custom_call", output_to_operand_aliasing={{}: (14, {})} | custom-call | flops 5368709120 | bytes 16777216 | tf_op jit(solution)/shard_map/project_attend/pallas_call | solution.py:134
  311.0 1.8 collective-permute-start.3
  313.8 11.1 %project_near.3.refs_4_ = f32[1024,256]{1,0:T(8,128)} custom-call(s32[6]{0:T(128)} %fusion.1.order_ref, bf16[1024,8192]{1,0:T(8,128)(2,1)} %tokens_ref.23, bf16[1024,2048]{1,0:T(8,128)(2,1)} %refs_0_.19, bf16[1024,2048]{1,0:T(8,128)(2,1)} %collective-permute-done.6.refs_1_, bf16[1024,256]{1,0:T(8,128)(2,1)} %copy-done.2, bf16[1024,256]{1,0:T(8,128)(2,1)} %copy-done.46, ...), custom_call_target="tpu_custom_call" | custom-call | flops 3221225472 | bytes 12582912 | tf_op jit(solution)/shard_map/project_near/pallas_call | solution.py:134
  326.8 9.8 %project_far_attend.2.refs_9_ = bf16[1024,2048]{1,0:T(8,128)(2,1)} custom-call(s32[4]{0:T(128)} %fusion.order_ref, bf16[1024,8192]{1,0:T(8,128)(2,1)} %tokens_ref.23, bf16[512,256]{1,0:T(8,128)(2,1)} %copy-done.49, bf16[512,256]{1,0:T(8,128)(2,1)} %copy-done.50, bf16[512,256]{1,0:T(8,128)(2,1)} %copy-done.56, ...), custom_call_target="tpu_custom_call", output_to_operand_aliasing={{}: (11, {})} | custom-call | flops 2147483648 | bytes 4194304 | tf_op jit(solution)/shard_map/project_far_attend/pallas_call | solution.py:134
  338.3 10.6 %project_near.2.refs_4_ = f32[1024,256]{1,0:T(8,128)} custom-call(s32[6]{0:T(128)} %fusion.1.order_ref, bf16[1024,8192]{1,0:T(8,128)(2,1)} %tokens_ref.23, bf16[1024,2048]{1,0:T(8,128)(2,1)} %refs_0_.19, bf16[1024,2048]{1,0:T(8,128)(2,1)} %collective-permute-done.6.refs_1_, bf16[1024,256]{1,0:T(8,128)(2,1)} %copy-done, bf16[1024,256]{1,0:T(8,128)(2,1)} %copy-done.44, ...), custom_call_target="tpu_custom_call" | custom-call | flops 3221225472 | bytes 12582912 | tf_op jit(solution)/shard_map/project_near/pallas_call | solution.py:134
  350.4 10.0 %project_far_attend.3 = bf16[1024,2048]{1,0:T(8,128)(2,1)} custom-call(s32[4]{0:T(128)} %fusion.order_ref, bf16[1024,8192]{1,0:T(8,128)(2,1)} %tokens_ref.23, bf16[512,256]{1,0:T(8,128)(2,1)} %copy-done.52, bf16[512,256]{1,0:T(8,128)(2,1)} %copy-done.53, bf16[512,256]{1,0:T(8,128)(2,1)} %copy-done.54, ...), custom_call_target="tpu_custom_call", output_to_operand_aliasing={{}: (11, {})} | custom-call | flops 2147483648 | bytes 4194304 | tf_op jit(solution)/shard_map/project_far_attend/pallas_call | solution.py:134
  (227 shorter events, 32.4 us)
Async XLA Ops:
  3.0 16.5 %collective-permute-start.9 = (bf16[1024,256]{1,0:T(8,128)(2,1)}, bf16[1024,256]{1,0:T(8,128)(2,1)S(1)}, u32[]{:S(2)}, u32[]{:S(2)}) collective-permute-start(bf16[1024,256]{1,0:T(8,128)(2,1)} %refs_0_.11), channel_id=1, source_target_pairs={{0,4},{4,0},{8,12},{12,8},{16,20},{20,16},{24,28},{28,24},{1,5},{5... | collective-permute-start | bytes 1572872 | tf_op jit(solution)/shard_map/ppermute | solution.py:196
  3.0 26.2 %collective-permute-start.19 = (bf16[1024,256]{1,0:T(8,128)(2,1)}, bf16[1024,256]{1,0:T(8,128)(2,1)S(1)}, u32[]{:S(2)}, u32[]{:S(2)}) collective-permute-start(bf16[1024,256]{1,0:T(8,128)(2,1)} %refs_0_.12), channel_id=1, source_target_pairs={{0,16},{4,20},{8,0},{12,4},{24,8},{28,12},{16,24},{20,28},{1,17},{... | collective-permute-start | bytes 1572872 | tf_op jit(solution)/shard_map/ppermute | solution.py:185
  5.0 24.3 %collective-permute-start.17 = (bf16[1024,256]{1,0:T(8,128)(2,1)}, bf16[1024,256]{1,0:T(8,128)(2,1)S(1)}, u32[]{:S(2)}, u32[]{:S(2)}) collective-permute-start(bf16[1024,256]{1,0:T(8,128)(2,1)} %refs_0_.12), channel_id=1, source_target_pairs={{0,8},{4,12},{8,24},{12,28},{24,16},{28,20},{16,0},{20,4},{1,9},{5... | collective-permute-start | bytes 1572872 | tf_op jit(solution)/shard_map/ppermute | solution.py:185
  18.0 20.4 %collective-permute-start.61 = (bf16[1024,256]{1,0:T(8,128)(2,1)S(1)}, bf16[1024,256]{1,0:T(8,128)(2,1)S(1)}, u32[]{:S(2)}, u32[]{:S(2)}) collective-permute-start(bf16[1024,256]{1,0:T(8,128)(2,1)S(1)} %get-tuple-element.5), channel_id=1, source_target_pairs={{0,8},{4,12},{8,24},{12,28},{24,16},{28,20},{16,0},{20,4},{1,9},{5... | collective-permute-start | bytes 1572872 | tf_op jit(solution)/shard_map/ppermute | solution.py:185
  19.5 20.9 %collective-permute-start.63 = (bf16[1024,256]{1,0:T(8,128)(2,1)S(1)}, bf16[1024,256]{1,0:T(8,128)(2,1)S(1)}, u32[]{:S(2)}, u32[]{:S(2)}) collective-permute-start(bf16[1024,256]{1,0:T(8,128)(2,1)S(1)} %get-tuple-element.5), channel_id=1, source_target_pairs={{0,16},{4,20},{8,0},{12,4},{24,8},{28,12},{16,24},{20,28},{1,17},{... | collective-permute-start | bytes 1572872 | tf_op jit(solution)/shard_map/ppermute | solution.py:185
  29.2 22.5 %collective-permute-start.57 = (bf16[1024,256]{1,0:T(8,128)(2,1)S(1)}, bf16[1024,256]{1,0:T(8,128)(2,1)S(1)}, u32[]{:S(2)}, u32[]{:S(2)}) collective-permute-start(bf16[1024,256]{1,0:T(8,128)(2,1)S(1)} %get-tuple-element.6), channel_id=1, source_target_pairs={{0,16},{4,20},{8,0},{12,4},{24,8},{28,12},{16,24},{20,28},{1,17},{... | collective-permute-start | bytes 1572872 | tf_op jit(solution)/shard_map/ppermute | solution.py:185
  29.3 23.9 %collective-permute-start.55 = (bf16[1024,256]{1,0:T(8,128)(2,1)S(1)}, bf16[1024,256]{1,0:T(8,128)(2,1)}, u32[]{:S(2)}, u32[]{:S(2)}) collective-permute-start(bf16[1024,256]{1,0:T(8,128)(2,1)S(1)} %get-tuple-element.6), channel_id=1, source_target_pairs={{0,8},{4,12},{8,24},{12,28},{24,16},{28,20},{16,0},{20,4},{1,9},{5... | collective-permute-start | bytes 1572872 | tf_op jit(solution)/shard_map/ppermute | solution.py:185
  31.3 29.7 %collective-permute-start.49 = (bf16[1024,256]{1,0:T(8,128)(2,1)S(1)}, bf16[1024,256]{1,0:T(8,128)(2,1)}, u32[]{:S(2)}, u32[]{:S(2)}) collective-permute-start(bf16[1024,256]{1,0:T(8,128)(2,1)S(1)} %get-tuple-element.7), channel_id=1, source_target_pairs={{0,8},{4,12},{8,24},{12,28},{24,16},{28,20},{16,0},{20,4},{1,9},{5... | collective-permute-start | bytes 1572872 | tf_op jit(solution)/shard_map/ppermute | solution.py:185
  38.4 24.6 %collective-permute-start.51 = (bf16[1024,256]{1,0:T(8,128)(2,1)S(1)}, bf16[1024,256]{1,0:T(8,128)(2,1)S(1)}, u32[]{:S(2)}, u32[]{:S(2)}) collective-permute-start(bf16[1024,256]{1,0:T(8,128)(2,1)S(1)} %get-tuple-element.7), channel_id=1, source_target_pairs={{0,16},{4,20},{8,0},{12,4},{24,8},{28,12},{16,24},{20,28},{1,17},{... | collective-permute-start | bytes 1572872 | tf_op jit(solution)/shard_map/ppermute | solution.py:185
  40.5 33.7 %collective-permute-start.45 = (bf16[1024,256]{1,0:T(8,128)(2,1)S(1)}, bf16[1024,256]{1,0:T(8,128)(2,1)S(1)}, u32[]{:S(2)}, u32[]{:S(2)}) collective-permute-start(bf16[1024,256]{1,0:T(8,128)(2,1)S(1)} %get-tuple-element.8), channel_id=1, source_target_pairs={{0,16},{4,20},{8,0},{12,4},{24,8},{28,12},{16,24},{20,28},{1,17},{... | collective-permute-start | bytes 1572872 | tf_op jit(solution)/shard_map/ppermute | solution.py:185
  51.7 22.5 %collective-permute-start.43 = (bf16[1024,256]{1,0:T(8,128)(2,1)S(1)}, bf16[1024,256]{1,0:T(8,128)(2,1)S(1)}, u32[]{:S(2)}, u32[]{:S(2)}) collective-permute-start(bf16[1024,256]{1,0:T(8,128)(2,1)S(1)} %get-tuple-element.8), channel_id=1, source_target_pairs={{0,8},{4,12},{8,24},{12,28},{24,16},{28,20},{16,0},{20,4},{1,9},{5... | collective-permute-start | bytes 1572872 | tf_op jit(solution)/shard_map/ppermute | solution.py:185
  53.2 144.5 %collective-permute-start.6 = (bf16[1024,2048]{1,0:T(8,128)(2,1)}, bf16[1024,2048]{1,0:T(8,128)(2,1)}, u32[]{:S(2)}, u32[]{:S(2)}) collective-permute-start(bf16[1024,2048]{1,0:T(8,128)(2,1)} %refs_0_.19), channel_id=1, source_target_pairs={{0,4},{4,0},{8,12},{12,8},{16,20},{20,16},{24,28},{28,24},{1,5},{5... | collective-permute-start | bytes 12582920 | tf_op jit(solution)/shard_map/ppermute | solution.py:199
  61.0 22.4 %collective-permute-start.37 = (bf16[1024,256]{1,0:T(8,128)(2,1)S(1)}, bf16[1024,256]{1,0:T(8,128)(2,1)S(1)}, u32[]{:S(2)}, u32[]{:S(2)}) collective-permute-start(bf16[1024,256]{1,0:T(8,128)(2,1)S(1)} %get-tuple-element.9), channel_id=1, source_target_pairs={{0,8},{4,12},{8,24},{12,28},{24,16},{28,20},{16,0},{20,4},{1,9},{5... | collective-permute-start | bytes 1572872 | tf_op jit(solution)/shard_map/ppermute | solution.py:185
  63.0 22.4 %collective-permute-start.39 = (bf16[1024,256]{1,0:T(8,128)(2,1)S(1)}, bf16[1024,256]{1,0:T(8,128)(2,1)S(1)}, u32[]{:S(2)}, u32[]{:S(2)}) collective-permute-start(bf16[1024,256]{1,0:T(8,128)(2,1)S(1)} %get-tuple-element.9), channel_id=1, source_target_pairs={{0,16},{4,20},{8,0},{12,4},{24,8},{28,12},{16,24},{20,28},{1,17},{... | collective-permute-start | bytes 1572872 | tf_op jit(solution)/shard_map/ppermute | solution.py:185
  74.2 22.5 %collective-permute-start.33 = (bf16[1024,256]{1,0:T(8,128)(2,1)S(1)}, bf16[1024,256]{1,0:T(8,128)(2,1)S(1)}, u32[]{:S(2)}, u32[]{:S(2)}) collective-permute-start(bf16[1024,256]{1,0:T(8,128)(2,1)S(1)} %get-tuple-element.10), channel_id=1, source_target_pairs={{0,16},{4,20},{8,0},{12,4},{24,8},{28,12},{16,24},{20,28},{1,17},{... | collective-permute-start | bytes 1572872 | tf_op jit(solution)/shard_map/ppermute | solution.py:185
  74.2 23.9 %collective-permute-start.23 = (bf16[1024,256]{1,0:T(8,128)(2,1)S(1)}, bf16[1024,256]{1,0:T(8,128)(2,1)S(1)}, u32[]{:S(2)}, u32[]{:S(2)}) collective-permute-start(bf16[1024,256]{1,0:T(8,128)(2,1)S(1)} %get-tuple-element.11), channel_id=1, source_target_pairs={{0,8},{4,12},{8,24},{12,28},{24,16},{28,20},{16,0},{20,4},{1,9},{5... | collective-permute-start | bytes 1572872 | tf_op jit(solution)/shard_map/ppermute | solution.py:185
  83.3 22.5 %collective-permute-start.31 = (bf16[1024,256]{1,0:T(8,128)(2,1)S(1)}, bf16[1024,256]{1,0:T(8,128)(2,1)S(1)}, u32[]{:S(2)}, u32[]{:S(2)}) collective-permute-start(bf16[1024,256]{1,0:T(8,128)(2,1)S(1)} %get-tuple-element.10), channel_id=1, source_target_pairs={{0,8},{4,12},{8,24},{12,28},{24,16},{28,20},{16,0},{20,4},{1,9},{5... | collective-permute-start | bytes 1572872 | tf_op jit(solution)/shard_map/ppermute | solution.py:185
  85.4 22.5 %collective-permute-start.25 = (bf16[1024,256]{1,0:T(8,128)(2,1)S(1)}, bf16[1024,256]{1,0:T(8,128)(2,1)S(1)}, u32[]{:S(2)}, u32[]{:S(2)}) collective-permute-start(bf16[1024,256]{1,0:T(8,128)(2,1)S(1)} %get-tuple-element.11), channel_id=1, source_target_pairs={{0,16},{4,20},{8,0},{12,4},{24,8},{28,12},{16,24},{20,28},{1,17},{... | collective-permute-start | bytes 1572872 | tf_op jit(solution)/shard_map/ppermute | solution.py:185
  96.7 20.4 %collective-permute-start = (bf16[1024,256]{1,0:T(8,128)(2,1)S(1)}, bf16[1024,256]{1,0:T(8,128)(2,1)S(1)}, u32[]{:S(2)}, u32[]{:S(2)}) collective-permute-start(bf16[1024,256]{1,0:T(8,128)(2,1)S(1)} %get-tuple-element.12), channel_id=1, source_target_pairs={{0,8},{4,12},{8,24},{12,28},{24,16},{28,20},{16,0},{20,4},{1,9},{5... | collective-permute-start | bytes 1572872 | tf_op jit(solution)/shard_map/ppermute | solution.py:185
  98.2 19.5 %collective-permute-start.2 = (bf16[1024,256]{1,0:T(8,128)(2,1)S(1)}, bf16[1024,256]{1,0:T(8,128)(2,1)S(1)}, u32[]{:S(2)}, u32[]{:S(2)}) collective-permute-start(bf16[1024,256]{1,0:T(8,128)(2,1)S(1)} %get-tuple-element.12), channel_id=1, source_target_pairs={{0,16},{4,20},{8,0},{12,4},{24,8},{28,12},{16,24},{20,28},{1,17},{... | collective-permute-start | bytes 1572872 | tf_op jit(solution)/shard_map/ppermute | solution.py:185
  105.8 16.9 %collective-permute-start.24 = (bf16[512,256]{1,0:T(8,128)(2,1)S(1)}, bf16[512,256]{1,0:T(8,128)(2,1)S(1)}, u32[]{:S(2)}, u32[]{:S(2)}) collective-permute-start(bf16[512,256]{1,0:T(8,128)(2,1)S(1)} %slice.50), channel_id=1, source_target_pairs={{0,8},{4,12},{8,24},{12,28},{24,16},{28,20},{16,0},{20,4},{1,9},{5... | collective-permute-start | bytes 786440 | tf_op jit(solution)/shard_map/ppermute | solution.py:193
  107.9 25.3 %collective-permute-start.14 = (bf16[1024,256]{1,0:T(8,128)(2,1)S(1)}, bf16[1024,256]{1,0:T(8,128)(2,1)}, u32[]{:S(2)}, u32[]{:S(2)}) collective-permute-start(bf16[1024,256]{1,0:T(8,128)(2,1)S(1)} %collective-permute-done.10.refs_2_), channel_id=1, source_target_pairs={{0,8},{4,12},{8,24},{12,28},{24,16},{28,20},{16,0},{20,4},{1,9},{5... | collective-permute-start | bytes 1572872 | tf_op jit(solution)/shard_map/ppermute | solution.py:188
  117.1 16.1 %collective-permute-start.11 = (bf16[1024,256]{1,0:T(8,128)(2,1)S(1)}, bf16[1024,256]{1,0:T(8,128)(2,1)S(1)}, u32[]{:S(2)}, u32[]{:S(2)}) collective-permute-start(bf16[1024,256]{1,0:T(8,128)(2,1)S(1)} %collective-permute-done.10.refs_2_), channel_id=1, source_target_pairs={{0,4},{4,0},{8,12},{12,8},{16,20},{20,16},{24,28},{28,24},{1,5},{5... | collective-permute-start | bytes 1572872 | tf_op jit(solution)/shard_map/ppermute | solution.py:186
  117.7 16.0 %collective-permute-start.13 = (bf16[1024,256]{1,0:T(8,128)(2,1)S(1)}, bf16[1024,256]{1,0:T(8,128)(2,1)S(1)}, u32[]{:S(2)}, u32[]{:S(2)}) collective-permute-start(bf16[1024,256]{1,0:T(8,128)(2,1)S(1)} %collective-permute-done.12.refs_4_), channel_id=1, source_target_pairs={{0,4},{4,0},{8,12},{12,8},{16,20},{20,16},{24,28},{28,24},{1,5},{5... | collective-permute-start | bytes 1572872 | tf_op jit(solution)/shard_map/ppermute | solution.py:186
  157.5 25.6 %collective-permute-start.52 = (bf16[1024,256]{1,0:T(8,128)(2,1)}, bf16[1024,256]{1,0:T(8,128)(2,1)}, u32[]{:S(2)}, u32[]{:S(2)}) collective-permute-start(bf16[1024,256]{1,0:T(8,128)(2,1)} %copy-done.14), channel_id=1, source_target_pairs={{0,4},{4,0},{8,12},{12,8},{16,20},{20,16},{24,28},{28,24},{1,5},{5... | collective-permute-start | bytes 1572872 | tf_op jit(solution)/shard_map/ppermute | solution.py:186
  162.5 20.9 %collective-permute-start.47 = (bf16[1024,256]{1,0:T(8,128)(2,1)S(1)}, bf16[1024,256]{1,0:T(8,128)(2,1)}, u32[]{:S(2)}, u32[]{:S(2)}) collective-permute-start(bf16[1024,256]{1,0:T(8,128)(2,1)S(1)} %collective-permute-done.45.refs_4_), channel_id=1, source_target_pairs={{0,16},{4,20},{8,0},{12,4},{24,8},{28,12},{16,24},{20,28},{1,17},{... | collective-permute-start | bytes 1572872 | tf_op jit(solution)/shard_map/ppermute | solution.py:190
  164.4 19.4 %collective-permute-start.22 = (bf16[1024,256]{1,0:T(8,128)(2,1)}, bf16[1024,256]{1,0:T(8,128)(2,1)}, u32[]{:S(2)}, u32[]{:S(2)}) collective-permute-start(bf16[1024,256]{1,0:T(8,128)(2,1)} %collective-permute-done.21.refs_6_), channel_id=1, source_target_pairs={{0,4},{4,0},{8,12},{12,8},{16,20},{20,16},{24,28},{28,24},{1,5},{5... | collective-permute-start | bytes 1572872 | tf_op jit(solution)/shard_map/ppermute | solution.py:194
  169.4 27.8 %collective-permute-start.66 = (bf16[1024,256]{1,0:T(8,128)(2,1)}, bf16[1024,256]{1,0:T(8,128)(2,1)S(1)}, u32[]{:S(2)}, u32[]{:S(2)}) collective-permute-start(bf16[1024,256]{1,0:T(8,128)(2,1)} %collective-permute-done.65.refs_6_), channel_id=1, source_target_pairs={{0,4},{4,0},{8,12},{12,8},{16,20},{20,16},{24,28},{28,24},{1,5},{5... | collective-permute-start | bytes 1572872 | tf_op jit(solution)/shard_map/ppermute | solution.py:194
  183.1 32.3 %collective-permute-start.46 = (bf16[1024,256]{1,0:T(8,128)(2,1)S(1)}, bf16[1024,256]{1,0:T(8,128)(2,1)S(1)}, u32[]{:S(2)}, u32[]{:S(2)}) collective-permute-start(bf16[1024,256]{1,0:T(8,128)(2,1)S(1)} %collective-permute-done.45.refs_4_), channel_id=1, source_target_pairs={{0,4},{4,0},{8,12},{12,8},{16,20},{20,16},{24,28},{28,24},{1,5},{5... | collective-permute-start | bytes 1572872 | tf_op jit(solution)/shard_map/ppermute | solution.py:186
  183.4 32.5 %collective-permute-start.44 = (bf16[1024,256]{1,0:T(8,128)(2,1)S(1)}, bf16[1024,256]{1,0:T(8,128)(2,1)S(1)}, u32[]{:S(2)}, u32[]{:S(2)}) collective-permute-start(bf16[1024,256]{1,0:T(8,128)(2,1)S(1)} %copy-done.11), channel_id=1, source_target_pairs={{0,4},{4,0},{8,12},{12,8},{16,20},{20,16},{24,28},{28,24},{1,5},{5... | collective-permute-start | bytes 1572872 | tf_op jit(solution)/shard_map/ppermute | solution.py:186
  183.7 34.1 %collective-permute-start.60 = (bf16[1024,256]{1,0:T(8,128)(2,1)S(1)}, bf16[1024,256]{1,0:T(8,128)(2,1)}, u32[]{:S(2)}, u32[]{:S(2)}) collective-permute-start(bf16[1024,256]{1,0:T(8,128)(2,1)S(1)} %copy-done.19), channel_id=1, source_target_pairs={{0,4},{4,0},{8,12},{12,8},{16,20},{20,16},{24,28},{28,24},{1,5},{5... | collective-permute-start | bytes 1572872 | tf_op jit(solution)/shard_map/ppermute | solution.py:194
  197.2 38.2 %collective-permute-start.41 = (bf16[1024,256]{1,0:T(8,128)(2,1)S(1)}, bf16[1024,256]{1,0:T(8,128)(2,1)S(1)}, u32[]{:S(2)}, u32[]{:S(2)}) collective-permute-start(bf16[1024,256]{1,0:T(8,128)(2,1)S(1)} %copy-done.7), channel_id=1, source_target_pairs={{0,8},{4,12},{8,24},{12,28},{24,16},{28,20},{16,0},{20,4},{1,9},{5... | collective-permute-start | bytes 1572872 | tf_op jit(solution)/shard_map/ppermute | solution.py:188
  197.7 38.3 %collective-permute-start.54 = (bf16[1024,256]{1,0:T(8,128)(2,1)}, bf16[1024,256]{1,0:T(8,128)(2,1)}, u32[]{:S(2)}, u32[]{:S(2)}) collective-permute-start(bf16[1024,256]{1,0:T(8,128)(2,1)} %collective-permute-done.53.refs_6_), channel_id=1, source_target_pairs={{0,4},{4,0},{8,12},{12,8},{16,20},{20,16},{24,28},{28,24},{1,5},{5... | collective-permute-start | bytes 1572872 | tf_op jit(solution)/shard_map/ppermute | solution.py:194
  215.5 38.6 %collective-permute-start.38 = (bf16[1024,256]{1,0:T(8,128)(2,1)S(1)}, bf16[1024,256]{1,0:T(8,128)(2,1)S(1)}, u32[]{:S(2)}, u32[]{:S(2)}) collective-permute-start(bf16[1024,256]{1,0:T(8,128)(2,1)S(1)} %copy-done.7), channel_id=1, source_target_pairs={{0,4},{4,0},{8,12},{12,8},{16,20},{20,16},{24,28},{28,24},{1,5},{5... | collective-permute-start | bytes 1572872 | tf_op jit(solution)/shard_map/ppermute | solution.py:186
  215.9 38.7 %collective-permute-start.35 = (bf16[1024,256]{1,0:T(8,128)(2,1)S(1)}, bf16[1024,256]{1,0:T(8,128)(2,1)S(1)}, u32[]{:S(2)}, u32[]{:S(2)}) collective-permute-start(bf16[1024,256]{1,0:T(8,128)(2,1)S(1)} %collective-permute-done.33.refs_4_), channel_id=1, source_target_pairs={{0,16},{4,20},{8,0},{12,4},{24,8},{28,12},{16,24},{20,28},{1,17},{... | collective-permute-start | bytes 1572872 | tf_op jit(solution)/shard_map/ppermute | solution.py:190
  217.8 36.9 %collective-permute-start.48 = (bf16[1024,256]{1,0:T(8,128)(2,1)}, bf16[1024,256]{1,0:T(8,128)(2,1)S(1)}, u32[]{:S(2)}, u32[]{:S(2)}) collective-permute-start(bf16[1024,256]{1,0:T(8,128)(2,1)} %collective-permute-done.47.refs_6_), channel_id=1, source_target_pairs={{0,4},{4,0},{8,12},{12,8},{16,20},{20,16},{24,28},{28,24},{1,5},{5... | collective-permute-start | bytes 1572872 | tf_op jit(solution)/shard_map/ppermute | solution.py:194
  235.4 37.8 %collective-permute-start.40 = (bf16[1024,256]{1,0:T(8,128)(2,1)S(1)}, bf16[1024,256]{1,0:T(8,128)(2,1)S(1)}, u32[]{:S(2)}, u32[]{:S(2)}) collective-permute-start(bf16[1024,256]{1,0:T(8,128)(2,1)S(1)} %copy-done.13), channel_id=1, source_target_pairs={{0,4},{4,0},{8,12},{12,8},{16,20},{20,16},{24,28},{28,24},{1,5},{5... | collective-permute-start | bytes 1572872 | tf_op jit(solution)/shard_map/ppermute | solution.py:186
  236.0 37.8 %collective-permute-start.42 = (bf16[1024,256]{1,0:T(8,128)(2,1)S(1)}, bf16[1024,256]{1,0:T(8,128)(2,1)}, u32[]{:S(2)}, u32[]{:S(2)}) collective-permute-start(bf16[1024,256]{1,0:T(8,128)(2,1)S(1)} %collective-permute-done.41.refs_6_), channel_id=1, source_target_pairs={{0,4},{4,0},{8,12},{12,8},{16,20},{20,16},{24,28},{28,24},{1,5},{5... | collective-permute-start | bytes 1572872 | tf_op jit(solution)/shard_map/ppermute | solution.py:194
  254.1 37.7 %collective-permute-start.34 = (bf16[1024,256]{1,0:T(8,128)(2,1)S(1)}, bf16[1024,256]{1,0:T(8,128)(2,1)S(1)}, u32[]{:S(2)}, u32[]{:S(2)}) collective-permute-start(bf16[1024,256]{1,0:T(8,128)(2,1)S(1)} %collective-permute-done.33.refs_4_), channel_id=1, source_target_pairs={{0,4},{4,0},{8,12},{12,8},{16,20},{20,16},{24,28},{28,24},{1,5},{5... | collective-permute-start | bytes 1572872 | tf_op jit(solution)/shard_map/ppermute | solution.py:186
  254.6 37.6 %collective-permute-start.32 = (bf16[1024,256]{1,0:T(8,128)(2,1)S(1)}, bf16[1024,256]{1,0:T(8,128)(2,1)S(1)}, u32[]{:S(2)}, u32[]{:S(2)}) collective-permute-start(bf16[1024,256]{1,0:T(8,128)(2,1)S(1)} %copy-done.9), channel_id=1, source_target_pairs={{0,4},{4,0},{8,12},{12,8},{16,20},{20,16},{24,28},{28,24},{1,5},{5... | collective-permute-start | bytes 1572872 | tf_op jit(solution)/shard_map/ppermute | solution.py:186
  254.8 37.7 %collective-permute-start.36 = (bf16[1024,256]{1,0:T(8,128)(2,1)S(1)}, bf16[1024,256]{1,0:T(8,128)(2,1)S(1)}, u32[]{:S(2)}, u32[]{:S(2)}) collective-permute-start(bf16[1024,256]{1,0:T(8,128)(2,1)S(1)} %collective-permute-done.35.refs_6_), channel_id=1, source_target_pairs={{0,4},{4,0},{8,12},{12,8},{16,20},{20,16},{24,28},{28,24},{1,5},{5... | collective-permute-start | bytes 1572872 | tf_op jit(solution)/shard_map/ppermute | solution.py:194
  273.3 39.5 %collective-permute-start.29 = (bf16[1024,256]{1,0:T(8,128)(2,1)S(1)}, bf16[1024,256]{1,0:T(8,128)(2,1)S(1)}, u32[]{:S(2)}, u32[]{:S(2)}) collective-permute-start(bf16[1024,256]{1,0:T(8,128)(2,1)S(1)} %collective-permute-done.23.refs_2_), channel_id=1, source_target_pairs={{0,4},{4,0},{8,12},{12,8},{16,20},{20,16},{24,28},{28,24},{1,5},{5... | collective-permute-start | bytes 1572872 | tf_op jit(solution)/shard_map/ppermute | solution.py:186
  273.8 39.2 %collective-permute-start.30 = (bf16[1024,256]{1,0:T(8,128)(2,1)S(1)}, bf16[1024,256]{1,0:T(8,128)(2,1)S(1)}, u32[]{:S(2)}, u32[]{:S(2)}) collective-permute-start(bf16[1024,256]{1,0:T(8,128)(2,1)S(1)} %collective-permute-done.25.refs_4_), channel_id=1, source_target_pairs={{0,4},{4,0},{8,12},{12,8},{16,20},{20,16},{24,28},{28,24},{1,5},{5... | collective-permute-start | bytes 1572872 | tf_op jit(solution)/shard_map/ppermute | solution.py:186
  291.9 19.2 %collective-permute-start.1 = (bf16[512,256]{1,0:T(8,128)(2,1)S(1)}, bf16[512,256]{1,0:T(8,128)(2,1)S(1)}, u32[]{:S(2)}, u32[]{:S(2)}) collective-permute-start(bf16[512,256]{1,0:T(8,128)(2,1)S(1)} %copy-done.59), channel_id=1, source_target_pairs={{0,8},{4,12},{8,24},{12,28},{24,16},{28,20},{16,0},{20,4},{1,9},{5... | collective-permute-start | bytes 786440 | tf_op jit(solution)/shard_map/ppermute | solution.py:193
  292.2 44.4 %collective-permute-start.7 = (bf16[1024,256]{1,0:T(8,128)(2,1)S(1)}, bf16[1024,256]{1,0:T(8,128)(2,1)S(1)}, u32[]{:S(2)}, u32[]{:S(2)}) collective-permute-start(bf16[1024,256]{1,0:T(8,128)(2,1)S(1)} %collective-permute-done.refs_2_), channel_id=1, source_target_pairs={{0,4},{4,0},{8,12},{12,8},{16,20},{20,16},{24,28},{28,24},{1,5},{5... | collective-permute-start | bytes 1572872 | tf_op jit(solution)/shard_map/ppermute | solution.py:186
  292.5 44.2 %collective-permute-start.8 = (bf16[1024,256]{1,0:T(8,128)(2,1)S(1)}, bf16[1024,256]{1,0:T(8,128)(2,1)S(1)}, u32[]{:S(2)}, u32[]{:S(2)}) collective-permute-start(bf16[1024,256]{1,0:T(8,128)(2,1)S(1)} %collective-permute-done.2.refs_4_), channel_id=1, source_target_pairs={{0,4},{4,0},{8,12},{12,8},{16,20},{20,16},{24,28},{28,24},{1,5},{5... | collective-permute-start | bytes 1572872 | tf_op jit(solution)/shard_map/ppermute | solution.py:186
  324.9 24.0 %collective-permute-start.4 = (bf16[512,256]{1,0:T(8,128)(2,1)S(1)}, bf16[512,256]{1,0:T(8,128)(2,1)S(1)}, u32[]{:S(2)}, u32[]{:S(2)}) collective-permute-start(bf16[512,256]{1,0:T(8,128)(2,1)S(1)} %collective-permute-done.1.refs_0_), channel_id=1, source_target_pairs={{0,4},{4,0},{8,12},{12,8},{16,20},{20,16},{24,28},{28,24},{1,5},{5... | collective-permute-start | bytes 786440 | tf_op jit(solution)/shard_map/ppermute | solution.py:194
  325.4 23.6 %collective-permute-start.5 = (bf16[512,256]{1,0:T(8,128)(2,1)S(1)}, bf16[512,256]{1,0:T(8,128)(2,1)S(1)}, u32[]{:S(2)}, u32[]{:S(2)}) collective-permute-start(bf16[512,256]{1,0:T(8,128)(2,1)S(1)} %collective-permute-done.3.refs_1_), channel_id=1, source_target_pairs={{0,4},{4,0},{8,12},{12,8},{16,20},{20,16},{24,28},{28,24},{1,5},{5... | collective-permute-start | bytes 786440 | tf_op jit(solution)/shard_map/ppermute | solution.py:194
  (79 other events, 2941.1 us)
